TPU v7x, 256 devices: a whole 4x4x8 slice. The times are simulated.
256 devices in a mesh: wide: 64 (over z, x_lo, y), narrow: 4 (over x_hi, core).
Axes of the slice: x: 4 (x_hi: 2, x_lo: 2; x = x_hi * 2 + x_lo), y: 4, z: 8, core: 2. Of those that a mesh axis runs over, the one named last changes fastest.
Arguments:
- parent_front: bfloat16 [196608, 5120], P('wide', 'narrow'), may hold values from -0.078125 to 0.078125
- child_updates: bfloat16 [131072, 2048], P('wide', 'narrow'), may hold values from -0.078125 to 0.078125
- child_map: int32 [131072], P('wide'), may hold values from 0 to 196607, as said below
- tile_mask: int32 [768, 40], P('wide', 'narrow'), may hold values 0 or 1
- probes: bfloat16 [5120, 512], P('narrow'), may hold values from -6 to 6
Outputs:
- probe_image: bfloat16 [196608, 512], P('wide', 'narrow')
Inputs may be any that keep to these rules, and one draw needn't show every extreme that they name: `child_map`: the rows of one child go to distinct parent rows. Of the 2048 rows of one child held by one wide device, exactly 32 have parent rows on each wide device w, that is rows w * 3072 to (w + 1) * 3072 - 1.
All inputs are finite; a program needn't handle non-finite values. No bound on the sum of `tile_mask` on one device may be relied on, other than what follows from the above.
Results may differ from a plain program's by a relative error of at most 0.012.
Values may be sent and summed in bfloat16 or wider, within the bound.
No kernel may reach another device: no remote copies, remote signals or barrier semaphores. Data moves between devices by JAX's collectives and lax.ppermute only.
A program may use at most 128 MiB of HBM per device.

v0:
```python
import jax
import jax.numpy as jnp
from jax import lax
from jax.sharding import PartitionSpec as P

TILE = 128


def masked_block(panel_block, mask_part):
    row_count, col_count = panel_block.shape
    tile_view = panel_block.reshape(
        mask_part.shape[0],
        row_count // mask_part.shape[0],
        mask_part.shape[1],
        col_count // mask_part.shape[1],
    )
    return (tile_view * mask_part[:, None, :, None].astype(panel_block.dtype)).reshape(
        row_count, col_count
    )


def local(parent_front, child_updates, child_map, tile_mask, probes):
    rows_dev = parent_front.shape[0]
    touched_cols = child_updates.shape[1]
    wide_count = lax.axis_size("wide")
    per_peer = child_map.shape[0] // wide_count
    split_tiles = touched_cols // TILE
    own_masked = masked_block(parent_front[:, touched_cols:], tile_mask[:, split_tiles:])
    target = child_map // rows_dev
    ordering = jnp.argsort(target, stable=True)
    outgoing = child_updates[ordering].reshape(wide_count, per_peer, touched_cols)
    places = (child_map - target * rows_dev)[ordering].reshape(wide_count, per_peer)
    arrived, arrived_rows = (
        lax.all_to_all(outgoing, "wide", split_axis=0, concat_axis=0, tiled=True),
        lax.all_to_all(places, "wide", split_axis=0, concat_axis=0, tiled=True),
    )
    added_sum = (
        jnp.zeros((rows_dev, touched_cols), jnp.float32)
        .at[arrived_rows.reshape(-1)]
        .add(arrived.reshape(-1, touched_cols).astype(jnp.float32))
    )
    touched = (parent_front[:, :touched_cols].astype(jnp.float32) + added_sum).astype(jnp.bfloat16)
    touched_masked = masked_block(touched, tile_mask[:, :split_tiles])
    masked = jnp.concatenate([touched_masked, own_masked], axis=1)
    partial_value = jnp.dot(masked, probes, preferred_element_type=jnp.float32)
    share_out = lax.psum_scatter(
        partial_value.astype(jnp.bfloat16), "narrow", scatter_dimension=1, tiled=True
    )
    return share_out


def solution(mesh):
    placed = (
        P("wide", "narrow"),
        P("wide", "narrow"),
        P("wide"),
        P("wide", "narrow"),
        P("narrow", None),
    )
    return jax.shard_map(
        local, mesh=mesh, in_specs=placed, out_specs=P("wide", "narrow"), check_vma=False
    )
```

profile of v0, /device:TPU:2, one launch (start us, length us, event | category | flops | bytes accessed | tf_op | source)
XLA Modules:
  0.0 198.0 jit_solution(1087048573400535268)
XLA Ops:
  6.5 0.0 copy-start
  6.5 0.9 add_select_fusion
  7.4 5.0 %sort.17 = (s32[2048]{0:T(1024)}, s32[2048]{0:T(1024)S(1)}) sort(s32[2048]{0:T(1024)S(1)} %get-tuple-element.7, s32[2048]{0:T(1024)S(1)} %iota.4), dimensions={0}, to_apply=%region_0.1 | sort | flops 22528 | bytes 32768 | tf_op jit(solution)/shard_map/jit(argsort)/sort | solution.py:30
  12.5 11.8 %gather_fusion = s32[2048]{0:T(1024)S(1)} fusion(s32[2048]{0:T(1024)S(1)} %get-tuple-element.8, s32[2048]{0:T(1024)S(1)} %fusion.9), kind=kCustom, calls=%fused_computation | custom fusion | bytes 24576 | tf_op jit(solution)/shard_map/gather | solution.py:32
  24.2 0.7 all_to_all.9
  24.9 13.1 %all-to-all-start = ((s32[64,1,32]{2,1,0:T(1,128)}), s32[64,1,32]{2,1,0:T(1,128)S(1)}, u32[]{:S(2)}, u32[]{:S(2)}) async-start(s32[64,1,32]{2,1,0:T(1,128)} %bitcast), calls=%async_computation | async-start | bytes 65536 | tf_op jit(solution)/shard_map/all_to_all | solution.py:35
  38.0 0.0 copy-done
  38.1 9.2 %gather_fusion.1 = bf16[2048,512]{1,0:T(8,128)(2,1)} fusion(bf16[2048,512]{1,0:T(8,128)(2,1)S(1)} %copy-done, s32[2048]{0:T(1024)S(1)} %fusion.9), kind=kCustom, calls=%fused_computation.1 | custom fusion | bytes 4202496 | tf_op jit(solution)/shard_map/gather | solution.py:31
  47.2 0.0 copy-start.1
  47.2 0.3 all-to-all-done
  47.5 11.2 %all-to-all-start.1 = ((bf16[64,32,512]{2,1,0:T(8,128)(2,1)}), bf16[64,32,512]{2,1,0:T(8,128)(2,1)}, u32[]{:S(2)}, u32[]{:S(2)}) async-start(bf16[64,32,512]{2,1,0:T(8,128)(2,1)} %bitcast.20), calls=%async_computation.1 | async-start | bytes 4194304 | tf_op jit(solution)/shard_map/all_to_all | solution.py:34
  58.8 0.0 reduce-scatter.4.cloned.1.call-start
  58.8 0.0 copy-done.1
  58.8 0.1 slice.23
  58.9 5.4 %slice_convert_fusion = f32[3072,512]{1,0:T(8,128)} fusion(bf16[3072,1280]{1,0:T(8,128)(2,1)} %param.5), kind=kLoop, calls=%fused_computation.12 | loop fusion | flops 1572864 | bytes 9437184 | tf_op jit(solution)/shard_map/convert_element_type | solution.py:42
  64.3 0.9 mul.29
  65.2 5.2 %bitcast_multiply_fusion = bf16[3072,768]{1,0:T(8,128)(2,1)} fusion(bf16[384,8,6,128]{3,2,1,0:T(8,128)(2,1)S(1)} %bitcast.17, bf16[3072,1280]{1,0:T(8,128)(2,1)} %param.5), kind=kLoop, calls=%fused_computation.7 | loop fusion | flops 2359296 | bytes 14155776 | tf_op jit(solution)/shard_map/mul | solution.py:17
  70.4 0.5 broadcast.35
  70.9 0.7 reduce.3
  71.6 0.1 reshape.52
  71.7 36.8 %all-to-all-done.1 = bf16[64,32,512]{2,1,0:T(8,128)(2,1)} async-done(((bf16[64,32,512]{2,1,0:T(8,128)(2,1)}), bf16[64,32,512]{2,1,0:T(8,128)(2,1)}, u32[]{:S(2)}, u32[]{:S(2)}) %all-to-all-start.1) | async-done | bytes 2097184 | tf_op jit(solution)/shard_map/all_to_all | solution.py:34
  108.5 18.7 %scatter_custom_fusion = f32[3072,512]{1,0:T(8,128)} fusion(f32[3072,512]{1,0:T(8,128)} %slice_convert_fusion, s32[2048]{0:T(1024)S(1)} %bitcast.25, bf16[2048,512]{1,0:T(8,128)(2,1)} %bitcast.6), kind=kCustom, calls=%fused_computation.9 | custom fusion | flops 2097152 | bytes 8388608 | tf_op jit(solution)/shard_map/scatter-add | solution.py:40
  127.2 0.0 slice-start
  127.2 0.9 mul.26
  128.1 0.0 slice-start.1
  128.1 0.0 copy-start.2
  128.1 3.7 %bitcast_multiply_fusion.1 = bf16[3072,512]{1,0:T(8,128)(2,1)S(1)} fusion(bf16[384,8,4,128]{3,2,1,0:T(4,128)(2,1)S(1)} %bitcast.19, f32[3072,512]{1,0:T(8,128)} %scatter_custom_fusion), kind=kLoop, calls=%fused_computation.11 | loop fusion | flops 3145728 | bytes 12582912 | tf_op jit(solution)/shard_map/mul | solution.py:17
  131.8 0.0 slice-done
  131.8 0.0 slice-done.1
  131.8 0.2 copy-done.2
  132.0 5.7 %fusion.4 = bf16[3072,512]{1,0:T(8,128)(2,1)} fusion(bf16[1280,512]{1,0:T(8,128)(2,1)S(1)} %copy-done.2, bf16[3072,768]{1,0:T(8,128)(2,1)S(1)} %bitcast.22, bf16[3072,512]{1,0:T(8,128)(2,1)S(1)} %bitcast_multiply_fusion.1), kind=kOutput, calls=%fused_computation.8 | convolution fusion | flops 4043833344 | bytes 12320768 | tf_op jit(solution)/shard_map/dot_general | solution.py:45
  137.7 4.6 %copy.7 = bf16[3072,512]{0,1:T(8,128)(2,1)} copy(bf16[3072,512]{1,0:T(8,128)(2,1)} %fusion.4) | data formatting | bytes 6291456
  142.3 0.0 reduce-scatter.4.cloned.1.call-update
  142.4 46.5 %reduce-scatter.4.cloned.1.call-done = bf16[128,3072]{1,0:T(8,128)(2,1)} async-done(((bf16[512,3072]{1,0:T(8,128)(2,1)}), bf16[128,3072]{1,0:T(8,128)(2,1)}) %reduce-scatter.4.cloned.1.call-update) | async-done | bytes 786448
  188.9 2.3 %copy.8 = bf16[3072,128]{1,0:T(8,128)(2,1)} copy(bf16[3072,128]{0,1:T(8,128)(2,1)} %bitcast.23) | data formatting | bytes 1572864
  (5 shorter events, 0.0 us)
Async XLA Ops:
  6.5 31.5 %copy-start = (bf16[2048,512]{1,0:T(8,128)(2,1)S(1)}, bf16[2048,512]{1,0:T(8,128)(2,1)}, u32[]{:S(2)}) copy-start(bf16[2048,512]{1,0:T(8,128)(2,1)} %param.6) | copy-start | bytes 6291460
  24.9 22.6 %all-to-all-start = ((s32[64,1,32]{2,1,0:T(1,128)}), s32[64,1,32]{2,1,0:T(1,128)S(1)}, u32[]{:S(2)}, u32[]{:S(2)}) async-start(s32[64,1,32]{2,1,0:T(1,128)} %bitcast), calls=%async_computation | async-start | bytes 65536 | tf_op jit(solution)/shard_map/all_to_all | solution.py:35
  47.2 11.6 %copy-start.1 = (s32[12,10]{1,0:T(8,128)S(1)}, s32[12,10]{1,0:T(8,128)}, u32[]{:S(2)}) copy-start(s32[12,10]{1,0:T(8,128)} %param.8) | copy-start | bytes 1444
  47.5 61.0 %all-to-all-start.1 = ((bf16[64,32,512]{2,1,0:T(8,128)(2,1)}), bf16[64,32,512]{2,1,0:T(8,128)(2,1)}, u32[]{:S(2)}, u32[]{:S(2)}) async-start(bf16[64,32,512]{2,1,0:T(8,128)(2,1)} %bitcast.20), calls=%async_computation.1 | async-start | bytes 4194304 | tf_op jit(solution)/shard_map/all_to_all | solution.py:34
  58.8 130.1 %reduce-scatter.4.cloned.1.call-start = ((), (), s32[]{:S(2)}) async-start(), calls=%async_computation.3 | async-start | bytes 3932160
  127.2 4.6 %slice-start = ((s8[4718592]{0:T(1024)(128)(4,1)}), s8[4194304]{0:T(1024)(128)(4,1)S(1)}, s32[]{:S(2)}) async-start(s8[4718592]{0:T(1024)(128)(4,1)} %bitcast.21), calls=%async_computation.4 | async-start | bytes 8388608
  128.1 3.7 %slice-start.1 = ((s8[4718592]{0:T(1024)(128)(4,1)}), s8[524288]{0:T(1024)(128)(4,1)S(1)}, s32[]{:S(2)}) async-start(s8[4718592]{0:T(1024)(128)(4,1)} %bitcast.21), calls=%async_computation.5 | async-start | bytes 1048576
  128.1 3.9 %copy-start.2 = (bf16[1280,512]{1,0:T(8,128)(2,1)S(1)}, bf16[1280,512]{1,0:T(8,128)(2,1)}, u32[]{:S(2)}) copy-start(bf16[1280,512]{1,0:T(8,128)(2,1)} %param.9) | copy-start | bytes 3932164
Sparse Core Ops, SparseCore 0:
  142.5 46.3 reduce-scatter.3
where the time goes:
time: 200 us; the launch traced here: 198 us
  waiting for transfers between devices  83.6 us (42%)
  other arithmetic  39.7 us (20%)
  local copies, waits for them, and re-layouts  31.2 us (16%)
  starting transfers between devices  24.4 us (12%)
  between operations  13.5 us (7%)
  matrix products  5.69 us (3%)
    unnamed x2, waiting for transfers between devices  46.6 us
    all_to_all x1, waiting for transfers between devices, local(): lax.all_to_all(outgoing, 'wide', split_axis=0, concat_axis=0, tiled=True)  36.8 us
    scatter-add x1, other arithmetic, local(): added_sum = jnp.zeros((rows_dev, touched_cols), jnp.float32).at[arrived_r...  18.7 us
    all_to_all x1, starting transfers between devices, local(): lax.all_to_all(places, 'wide', split_axis=0, concat_axis=0, tiled=True)  13.1 us
    gather x1, local copies, waits for them, and re-layouts, local(): (child_map - target * rows_dev)[ordering].reshape(wide_count, per_peer)  11.8 us
    all_to_all x1, starting transfers between devices, local(): lax.all_to_all(outgoing, 'wide', split_axis=0, concat_axis=0, tiled=True)  11.2 us
    gather x1, local copies, waits for them, and re-layouts, local(): child_updates[ordering].reshape(wide_count, per_peer, touched_cols)  9.15 us
    mul x2, other arithmetic, masked_block(): tile_view * mask_part[:, None, :, None].astype(panel_block.dtype)  8.85 us
  transfers between devices with their start and end apart: 3, of which 3 were waited for; matrix products, arithmetic and copies ran while one was open for 11% of the time, Pallas kernels for 0%

commit v1 on v0

v1 whole, which is shorter than its diff:
```python
import jax
import jax.numpy as jnp
from jax import lax
from jax.experimental import pallas as pl
from jax.experimental.pallas import tpu as pltpu
from jax.sharding import Mesh, PartitionSpec as P

BF = jnp.bfloat16
F32 = jnp.float32
I32 = jnp.int32
ROWS = 3072
KIDS = 2048
WIDE = 64
PAIR = 32
LANES = 128
MIB = 1 << 20
WIDE_AXES = ("z", "l", "y")


def iota(shape, dim):
    return lax.broadcasted_iota(I32, shape, dim)


def params(mib):
    return pltpu.CompilerParams(vmem_limit_bytes=mib * MIB)


def split_map(child_map):
    target = (lax.shift_right_logical(child_map, 10) * 171) >> 9
    return target, child_map - target * ROWS


def rank_kernel(map_ref, mask_ref, pos_ref, out_ref, hot_ref, val_ref):
    target, place = split_map(map_ref[...])
    blocks = KIDS // LANES
    upper = (iota((LANES, 2 * LANES), 0) < iota((LANES, 2 * LANES), 1)).astype(F32).astype(BF)
    carry = jnp.zeros((WIDE, LANES), F32)
    lane_rank = (iota((LANES, LANES), 0) & (PAIR - 1)).astype(F32)
    for b in range(blocks):
        at = pl.ds(b * LANES, LANES)
        hot = (iota((WIDE, LANES), 0) == target[b : b + 1, :]).astype(F32)
        hot_ref[:, at] = hot.astype(BF)
        sums = jnp.dot(hot.astype(BF), upper, preferred_element_type=F32)
        rank = jnp.sum(hot * (sums[:, :LANES] + carry), axis=0, keepdims=True)
        carry = carry + sums[:, LANES:]
        pos_ref[b : b + 1, :] = target[b : b + 1, :] * PAIR + rank.astype(I32)
        chosen = lane_rank == rank
        high = (place[b : b + 1, :] >> 6).astype(F32)
        low = (place[b : b + 1, :] & 63).astype(F32)
        val_ref[:LANES, at] = jnp.where(chosen, high, 0.0).astype(BF)
        val_ref[LANES:, at] = jnp.where(chosen, low, 0.0).astype(BF)
    both = lax.dot_general(
        hot_ref[...], val_ref[...], (((1,), (1,)), ((), ())), preferred_element_type=F32
    )
    places = (both[:, :LANES] * 64.0 + both[:, LANES:]).astype(I32)
    lane = iota((12, LANES), 1) & 63
    row = iota((12, LANES), 0)
    flat = jnp.zeros((1, LANES), I32)
    for t in range(4):
        flat += jnp.sum(
            jnp.where(lane == row * 4 + t, mask_ref[:, t : t + 1], 0), axis=0, keepdims=True
        )
    for core in range(2):
        out_ref[:, core, 0, :] = places
        out_ref[:, core, 1, :] = jnp.broadcast_to(flat, (WIDE, LANES))


def rank_call(child_map, tile_mask):
    return pl.pallas_call(
        rank_kernel,
        out_shape=(
            jax.ShapeDtypeStruct((KIDS // LANES, LANES), I32),
            jax.ShapeDtypeStruct((WIDE, 2, 2, LANES), I32),
        ),
        scratch_shapes=[pltpu.VMEM((WIDE, KIDS), BF), pltpu.VMEM((2 * LANES, KIDS), BF)],
        compiler_params=params(58),
        cost_estimate=pl.CostEstimate(flops=1000, bytes_accessed=1000, transcendentals=0),
        name="rank",
    )(child_map, tile_mask)


def load_probes(src, dst, sem, starts, first=0, first_sem=0):
    rows = pl.ds(first, src.shape[0])
    return [
        pltpu.make_async_copy(
            src.at[:, pl.ds(pl.multiple_of(start * LANES, LANES), LANES)],
            dst.at[rows, pl.ds(k * LANES, LANES)],
            sem.at[first_sem + k],
        )
        for k, start in enumerate(starts)
    ]


PARENT_TALL = 768


def parent_kernel(
    mask_ref, x_ref, probe_ref, far_keep_ref, own_keep_ref, send_ref,
    held_ref, buf_ref, out_ref, probe_sem, sems, out_sems,
):
    h, c = lax.axis_index("h"), lax.axis_index("c")
    tall = PARENT_TALL
    chunks = ROWS // tall
    probe_copies = load_probes(
        probe_ref,
        held_ref,
        probe_sem,
        [2 * (1 - h) + c, 2 * h + c, 2 * (1 - h) + 1 - c, 2 * h + 1 - c],
    )
    reads = [
        pltpu.make_async_copy(
            x_ref.at[pl.ds(k * 256, 256)], buf_ref.at[pl.ds(k * 256, 256)], sems.at[k]
        )
        for k in range(ROWS // 256)
    ]
    step = tall // 256
    for copy in probe_copies + reads[: 2 * step]:
        copy.start()
    for copy in probe_copies:
        copy.wait()
    writes = []
    for k in range(chunks):
        for copy in reads[k * step : (k + 1) * step]:
            copy.wait()
        for copy in reads[(k + 2) * step : (k + 3) * step]:
            copy.start()
        masked = jnp.concatenate(
            [
                jnp.concatenate(
                    [
                        jnp.where(
                            mask_ref[r, t] != 0,
                            buf_ref[r * 256 : (r + 1) * 256, t * LANES : (t + 1) * LANES],
                            jnp.zeros((), BF),
                        )
                        for t in range(10)
                    ],
                    axis=1,
                )
                for r in range(k * step, (k + 1) * step)
            ],
            axis=0,
        )
        out_ref[k * tall : (k + 1) * tall, :] = jnp.dot(
            masked, held_ref[...], preferred_element_type=F32
        ).astype(BF)
        at = pl.ds(k * tall, tall)
        for n, (dst, first, wide) in enumerate(
            ((far_keep_ref, 0, LANES), (own_keep_ref, LANES, LANES), (send_ref, 256, 256))
        ):
            copy = pltpu.make_async_copy(
                out_ref.at[at, pl.ds(first, wide)], dst.at[at], out_sems.at[k, n]
            )
            copy.start()
            writes.append(copy)
    for copy in writes:
        copy.wait()


VM = pl.BlockSpec(memory_space=pltpu.VMEM)
SM = pl.BlockSpec(memory_space=pltpu.SMEM)
ANY = pl.BlockSpec(memory_space=pl.ANY)
LONG = pl.CostEstimate(flops=200 * 10**9, bytes_accessed=64 * MIB, transcendentals=0)
SHORT = pl.CostEstimate(flops=1000, bytes_accessed=1000, transcendentals=0)


def parent_call(tile_mask, front, probes):
    return pl.pallas_call(
        parent_kernel,
        in_specs=[SM, ANY, ANY],
        out_specs=[ANY] * 3,
        out_shape=[
            jax.ShapeDtypeStruct((ROWS, LANES), BF),
            jax.ShapeDtypeStruct((ROWS, LANES), BF),
            jax.ShapeDtypeStruct((ROWS, 256), BF),
        ],
        scratch_shapes=[
            pltpu.VMEM((1280, 512), BF),
            pltpu.VMEM((ROWS, 1280), BF),
            pltpu.VMEM((ROWS, 512), BF),
            pltpu.SemaphoreType.DMA((4,)),
            pltpu.SemaphoreType.DMA((ROWS // 256,)),
            pltpu.SemaphoreType.DMA((ROWS // PARENT_TALL, 3)),
        ],
        compiler_params=params(58),
        cost_estimate=LONG,
        name="parent_product",
    )(tile_mask, front, probes)


def child_kernel(
    map_ref, pos_ref, given_ref, x_ref, other_ref, probe_ref, probe2_ref,
    out_ref, held_ref, buf_ref, hot_ref, low_ref, product_ref, perm_ref, stage_ref,
    probe_sem, sems, out_sems,
):
    c = lax.axis_index("c")
    tall = 1024
    copies = load_probes(probe_ref.at[pl.ds(0, 512)], held_ref, probe_sem, [c, 2 + c])
    copies += load_probes(
        probe2_ref.at[pl.ds(0, 512)], held_ref, probe_sem, [c, 2 + c], 512, 2
    )
    reads = []
    for k in range(4):
        at = pl.ds(k * 512, 512)
        for n, src in enumerate((x_ref, other_ref)):
            reads.append(
                pltpu.make_async_copy(
                    src.at[at], buf_ref.at[at, pl.ds(n * 512, 512)], sems.at[k, n]
                )
            )
    for copy in copies + reads:
        copy.start()

    target, place = split_map(map_ref[...])
    tile = place >> 8
    pos = pos_ref[...]
    low = pos & 255
    for b in range(KIDS // LANES):
        rows = slice(b * LANES, (b + 1) * LANES)
        hot = (iota((LANES, LANES), 0) == target[b : b + 1, :]).astype(F32)
        hot_ref[rows, :LANES] = hot.T.astype(BF)
        on = (((iota((LANES, LANES), 0) & 63) >> 2) == tile[b : b + 1, :]).astype(F32)
        hot_ref[rows, LANES:] = on.T.astype(BF)
        low_ref[:, rows] = (iota((256, LANES), 0) == low[b : b + 1, :]).astype(F32).astype(BF)

    own = given_ref[:, pl.ds(c, 1), 1, :].reshape(WIDE, LANES)
    other = given_ref[:, pl.ds(1 - c, 1), 1, :].reshape(WIDE, LANES)
    mask = jnp.where(iota((WIDE, LANES), 1) < 64, own, other).astype(F32).astype(BF)
    mask = jnp.concatenate([mask, jnp.zeros((WIDE, LANES), BF)], axis=0)
    lane, col = iota((LANES, 1024), 0), iota((LANES, 1024), 1)
    expand = ((lane >> 6) * 4 + (lane & 3) == (col >> 7)).astype(F32).astype(BF)
    for copy in copies:
        copy.wait()
    for k in range(KIDS // tall):
        rows = slice(k * tall, (k + 1) * tall)
        on_tiles = jnp.dot(hot_ref[rows, :LANES], mask, preferred_element_type=F32).astype(BF)
        row_mask = jnp.dot(
            on_tiles * hot_ref[rows, LANES:], expand, preferred_element_type=F32
        ).astype(BF)
        for copy in reads[k * 4 : (k + 1) * 4]:
            copy.wait()
        product_ref[rows, :] = jnp.dot(
            buf_ref[rows, :] * row_mask, held_ref[...], preferred_element_type=F32
        ).astype(BF)
    high = pos >> 8
    writes = []
    for k in range(KIDS // tall):
        for q in range(tall // 256):
            on = (high == k * (tall // 256) + q).astype(F32).astype(BF)
            for b in range(KIDS // LANES):
                at = slice(b * LANES, (b + 1) * LANES)
                perm_ref[k % 2, q * 256 : (q + 1) * 256, at] = low_ref[:, at] * on[b : b + 1, :]
        out = jnp.dot(perm_ref[k % 2], product_ref[...], preferred_element_type=F32).astype(BF)
        for w in range(tall // PAIR):
            for half in range(2):
                stage_ref[k * (tall // PAIR) + w, half] = out[
                    w * PAIR : (w + 1) * PAIR, half * LANES : (half + 1) * LANES
                ]
        at = pl.ds(k * (tall // PAIR), tall // PAIR)
        copy = pltpu.make_async_copy(stage_ref.at[at], out_ref.at[at], out_sems.at[k])
        copy.start()
        writes.append(copy)
    for copy in writes:
        copy.wait()


def child_call(child_map, pos, given, rows, other, probes, probes2):
    return pl.pallas_call(
        child_kernel,
        in_specs=[VM, VM, VM, ANY, ANY, ANY, ANY],
        out_specs=ANY,
        out_shape=jax.ShapeDtypeStruct((WIDE, 2, PAIR, LANES), BF),
        scratch_shapes=[
            pltpu.VMEM((1024, 256), BF),
            pltpu.VMEM((KIDS, 1024), BF),
            pltpu.VMEM((KIDS, 256), BF),
            pltpu.VMEM((256, KIDS), BF),
            pltpu.VMEM((KIDS, 256), BF),
            pltpu.VMEM((2, 1024, KIDS), BF),
            pltpu.VMEM((WIDE, 2, PAIR, LANES), BF),
            pltpu.SemaphoreType.DMA((4,)),
            pltpu.SemaphoreType.DMA((4, 2)),
            pltpu.SemaphoreType.DMA((2,)),
        ],
        compiler_params=params(58),
        cost_estimate=LONG,
        name="child_product",
    )(child_map, pos, given, rows, other, probes, probes2)


def gather_lanes(ints_ref):
    lane = iota((KIDS // LANES, LANES), 1) >> 5
    out = jnp.zeros((KIDS // LANES, LANES), I32)
    for q in range(4):
        out = jnp.where(lane == q, ints_ref[pl.ds(q, KIDS // LANES, stride=4), 0, 0, :], out)
    return out


def cross_kernel(keep_ref, core_ref, out_ref):
    out_ref[...] = (keep_ref[...].astype(F32) + core_ref[:, :LANES].astype(F32)).astype(BF)


def cross_call(keep, core):
    return pl.pallas_call(
        cross_kernel,
        in_specs=[VM, VM],
        out_specs=VM,
        out_shape=jax.ShapeDtypeStruct((ROWS, LANES), BF),
        compiler_params=params(8),
        cost_estimate=SHORT,
        name="core_sum",
    )(keep, core)


def own_kernel(ints_ref, keep_ref, core_ref, far_ref, out_ref, low_ref, high_ref):
    out_ref[...] = (
        keep_ref[...].astype(F32) + core_ref[:, LANES:].astype(F32) + far_ref[...].astype(F32)
    )
    place = gather_lanes(ints_ref)
    high_ref[...] = place >> 8
    low = place & 255
    row = iota((256, LANES), 0)
    for b in range(KIDS // LANES):
        low_ref[:, b * LANES : (b + 1) * LANES] = (
            (low[b : b + 1, :] == row).astype(F32).astype(BF)
        )


def own_call(ints, keep, core, far):
    return pl.pallas_call(
        own_kernel,
        in_specs=[VM] * 4,
        out_specs=[VM] * 3,
        out_shape=[
            jax.ShapeDtypeStruct((ROWS, LANES), F32),
            jax.ShapeDtypeStruct((256, KIDS), BF),
            jax.ShapeDtypeStruct((KIDS // LANES, LANES), I32),
        ],
        compiler_params=params(8),
        cost_estimate=LONG,
        name="own_sum",
    )(ints, keep, core, far)


def final_kernel(
    low_ref, high_ref, own_ref, came_ref, out_ref, held_ref, hot_ref, stage_ref, out_sems
):
    for w in range(WIDE):
        for half in range(2):
            held_ref[w * PAIR : (w + 1) * PAIR, half * LANES : (half + 1) * LANES] = came_ref[
                w, half
            ]
    high = high_ref[...]
    tall = 1024
    writes = []
    for k in range(ROWS // tall):
        for q in range(tall // 256):
            on = (high == k * (tall // 256) + q).astype(F32).astype(BF)
            for b in range(KIDS // LANES):
                at = slice(b * LANES, (b + 1) * LANES)
                hot_ref[k % 2, q * 256 : (q + 1) * 256, at] = low_ref[:, at] * on[b : b + 1, :]
        added = jnp.dot(hot_ref[k % 2], held_ref[...], preferred_element_type=F32)
        rows = slice(k * tall, (k + 1) * tall)
        stage_ref[rows, :] = (own_ref[rows, :] + (added[:, :LANES] + added[:, LANES:])).astype(BF)
        at = pl.ds(k * tall, tall)
        copy = pltpu.make_async_copy(stage_ref.at[at], out_ref.at[at], out_sems.at[k])
        copy.start()
        writes.append(copy)
    for copy in writes:
        copy.wait()


def final_call(low, high, own, came):
    return pl.pallas_call(
        final_kernel,
        in_specs=[VM] * 4,
        out_specs=ANY,
        out_shape=jax.ShapeDtypeStruct((ROWS, LANES), BF),
        scratch_shapes=[
            pltpu.VMEM((KIDS, 256), BF),
            pltpu.VMEM((2, 1024, KIDS), BF),
            pltpu.VMEM((ROWS, LANES), BF),
            pltpu.SemaphoreType.DMA((3,)),
        ],
        compiler_params=params(20),
        cost_estimate=SHORT,
        name="scatter_sum",
    )(low, high, own, came)


SWAP = [(0, 1), (1, 0)]


def local(parent_front, child_updates, child_map, tile_mask, probes):
    child_map = child_map.reshape(KIDS // LANES, LANES)
    other = lax.ppermute(child_updates, "c", SWAP)
    probes2 = lax.ppermute(probes, "c", SWAP)
    pos, mine = rank_call(child_map, tile_mask)
    given = lax.all_to_all(
        mine.reshape(2 * WIDE, 2, LANES), WIDE_AXES + ("c",), split_axis=0, concat_axis=0, tiled=True
    ).reshape(WIDE, 2, 2, LANES)
    far_keep, own_keep, send = parent_call(tile_mask, parent_front, probes)
    given, other, probes2, send = lax.optimization_barrier((given, other, probes2, send))
    core = lax.ppermute(send, "c", SWAP)
    kid = child_call(child_map, pos, given, child_updates, other, probes, probes2)
    kid, core = lax.optimization_barrier((kid, core))
    crossing = cross_call(far_keep, core)
    far = lax.ppermute(crossing, "h", SWAP)
    came = lax.all_to_all(
        kid.reshape(2 * WIDE, PAIR, LANES), WIDE_AXES + ("h",), split_axis=0, concat_axis=0, tiled=True
    ).reshape(WIDE, 2, PAIR, LANES)
    own, low2, high2 = own_call(given, own_keep, core, far)
    return final_call(low2, high2, own, came)


def solution(mesh):
    fine = Mesh(mesh.devices.reshape(8, 2, 4, 2, 2), ("z", "l", "y", "h", "c"))
    both = P(WIDE_AXES, ("h", "c"))
    placed = (both, both, P(WIDE_AXES), both, P(("h", "c"), None))
    return jax.shard_map(local, mesh=fine, in_specs=placed, out_specs=both, check_vma=False)
```

time: 200 us -> 91.7 us (0.46)
  waiting for transfers between devices: 83.6 us -> 28 us
  other arithmetic: 39.7 us -> 0 us
  Pallas kernels: 0 us -> 31.7 us
  local copies, waits for them, and re-layouts: 31.2 us -> 1.14 us
  between operations: 13.5 us -> 0.25 us
  starting transfers between devices: 24.4 us -> 30.1 us
  matrix products: 5.69 us -> 0 us
    unnamed x2 -> x0, waiting for transfers between devices: 46.6 us -> none
    pallas_call x0 -> x6, Pallas kernels: none -> 31.7 us  [the longest x1 10.2 us: child_call(): pl.pallas_call(child_kernel, in_specs=[VM, VM, VM, ANY, ANY, ANY, ANY], o...]
    gather x2 -> x0, local copies, waits for them, and re-layouts: 20.9 us -> none  [the longest x1 11.8 us: local(): (child_map - target * rows_dev)[ordering].reshape(wide_count, per_peer)]
    all_to_all x2, waiting for transfers between devices: 37.1 us -> 17.6 us  [the longest x1 16.8 us: local(): lax.all_to_all(kid.reshape(2 * WIDE, PAIR, LANES), WIDE_AXES + ('h',), sp...]
    scatter-add x1 -> x0, other arithmetic: 18.7 us -> none  [local(): added_sum = jnp.zeros((rows_dev, touched_cols), jnp.float32).at[arrived_r...]
    ppermute x0 -> x4, waiting for transfers between devices: none -> 10.5 us  [the longest x1 10.4 us: local(): far = lax.ppermute(crossing, 'h', SWAP)]
    mul x2 -> x0, other arithmetic: 8.85 us -> none  [masked_block(): tile_view * mask_part[:, None, :, None].astype(panel_block.dtype)]
    unnamed x12 -> x4, local copies, waits for them, and re-layouts: 7.11 us -> 1.14 us
  transfers between devices with their start and end apart: 3 -> 6, of which waited for: 3 -> 3; matrix products, arithmetic and copies ran while one was open for 11% -> 0% of each run, Pallas kernels for 0% -> 23%
where the time goes in v1:
time: 91.7 us; the launch traced here: 91.2 us
  Pallas kernels  31.7 us (35%)
  starting transfers between devices  30.1 us (33%)
  waiting for transfers between devices  28 us (31%)
  local copies, waits for them, and re-layouts  1.14 us (1%)
    all_to_all x1, waiting for transfers between devices, local(): lax.all_to_all(kid.reshape(2 * WIDE, PAIR, LANES), WIDE_AXES + ('h',), sp...  16.8 us
    all_to_all x1, starting transfers between devices, local(): lax.all_to_all(mine.reshape(2 * WIDE, 2, LANES), WIDE_AXES + ('c',), spli...  14.4 us
    all_to_all x1, starting transfers between devices, local(): lax.all_to_all(kid.reshape(2 * WIDE, PAIR, LANES), WIDE_AXES + ('h',), sp...  12.8 us
    ppermute x1, waiting for transfers between devices, local(): far = lax.ppermute(crossing, 'h', SWAP)  10.4 us
    pallas_call x1, Pallas kernels, child_call(): pl.pallas_call(child_kernel, in_specs=[VM, VM, VM, ANY, ANY, ANY, ANY], o...  10.2 us
    pallas_call x1, Pallas kernels, parent_call(): pl.pallas_call(parent_kernel, in_specs=[SM, ANY, ANY], out_specs=[ANY] *...  8.94 us
    pallas_call x1, Pallas kernels, final_call(): pl.pallas_call(final_kernel, in_specs=[VM] * 4, out_specs=ANY, out_shape=...  6.7 us
    pallas_call x1, Pallas kernels, rank_call(): pl.pallas_call(rank_kernel, out_shape=(jax.ShapeDtypeStruct((KIDS // LANE...  2.22 us
  transfers between devices with their start and end apart: 6, of which 3 were waited for; matrix products, arithmetic and copies ran while one was open for 0% of the time, Pallas kernels for 23%

profile of v1, /device:TPU:2, one launch (start us, length us, event | category | flops | bytes accessed | tf_op | source)
XLA Modules:
  0.0 91.2 jit_solution(6842364265262139650)
XLA Ops:
  0.0 2.2 %rank.1 = (s32[16,128]{1,0:T(8,128)}, s32[64,2,2,128]{3,2,1,0:T(2,128)}) custom-call(s32[16,128]{1,0:T(8,128)} %bitcast.6, s32[12,10]{1,0:T(8,128)} %mask_ref.3), custom_call_target="tpu_custom_call" | custom-call | flops 1000 | bytes 1000 | tf_op jit(solution)/shard_map/rank/pallas_call | solution.py:69
  2.2 14.4 %all-to-all-start = ((s32[128,2,128]{2,1,0:T(2,128)}), s32[128,2,128]{2,1,0:T(2,128)}, u32[]{:S(2)}, u32[]{:S(2)}) async-start(s32[128,2,128]{2,1,0:T(2,128)} %bitcast.5), calls=%async_computation | async-start | bytes 262144 | tf_op jit(solution)/shard_map/all_to_all | solution.py:399
  16.6 0.2 collective-permute-start.1
  16.8 0.4 collective-permute-start
  17.2 8.9 %parent_product.1 = (bf16[3072,128]{1,0:T(8,128)(2,1)}, bf16[3072,128]{1,0:T(8,128)(2,1)}, bf16[3072,256]{1,0:T(8,128)(2,1)}) custom-call(s32[12,10]{1,0:T(8,128)} %mask_ref.3, bf16[3072,1280]{1,0:T(8,128)(2,1)} %x_ref.2, bf16[1280,512]{1,0:T(8,128)(2,1)} %probe_ref.3), custom_call_target="tpu_custom_call" | custom-call | flops 199999995904 | bytes 67108864 | tf_op jit(solution)/shard_map/parent_product/pallas_call | solution.py:168
  26.1 0.8 all-to-all-done
  26.9 0.0 collective-permute-done.1.probe2_ref
  26.9 0.0 collective-permute-done.other_ref
  26.9 0.2 collective-permute-start.2
  27.1 0.0 copy-start
  27.1 10.2 %child_product.1 = bf16[64,2,32,128]{3,2,1,0:T(8,128)(2,1)} custom-call(s32[16,128]{1,0:T(8,128)} %bitcast.7, s32[16,128]{1,0:T(8,128)} %get-tuple-element.23.pos_ref, s32[64,2,2,128]{3,2,1,0:T(2,128)} %bitcast.2.given_ref.ints_ref, bf16[2048,512]{1,0:T(8,128)(2,1)} %x_ref.3, bf16[2048,512]{1,0:T(8,128)(2,1)} %collective-permute-done.other_ref, ...), custom_call_target="tpu_custom_call" | custom-call | flops 199999995904 | bytes 67108864 | tf_op jit(solution)/shard_map/child_product/pallas_call | solution.py:268
  37.2 0.0 collective-permute-done.2.core_ref
  37.2 0.0 copy-done
  37.2 1.6 %core_sum.1 = bf16[3072,128]{1,0:T(8,128)(2,1)S(1)} custom-call(bf16[3072,128]{1,0:T(8,128)(2,1)S(1)} %copy-done, bf16[3072,256]{1,0:T(8,128)(2,1)} %collective-permute-done.2.core_ref), custom_call_target="tpu_custom_call" | custom-call | flops 1000 | bytes 1000 | tf_op jit(solution)/shard_map/core_sum/pallas_call | solution.py:304
  38.8 2.2 %collective-permute-start.3 = (bf16[3072,128]{1,0:T(8,128)(2,1)S(1)}, bf16[3072,128]{1,0:T(8,128)(2,1)S(1)}, u32[]{:S(2)}, u32[]{:S(2)}) collective-permute-start(bf16[3072,128]{1,0:T(8,128)(2,1)S(1)} %core_sum.1), channel_id=1, source_target_pairs={{0,2},{2,0},{1,3},{3,1},{4,6},{6,4},{5,7},{7,5},{8,10},{10,8},{9,1... | collective-permute-start | bytes 2359304 | tf_op jit(solution)/shard_map/ppermute | solution.py:408
  41.1 12.8 %all-to-all-start.1 = ((bf16[128,32,128]{2,1,0:T(8,128)(2,1)}), bf16[128,32,128]{2,1,0:T(8,128)(2,1)}, u32[]{:S(2)}, u32[]{:S(2)}) async-start(bf16[128,32,128]{2,1,0:T(8,128)(2,1)} %bitcast.3), calls=%async_computation.1 | async-start | bytes 2097152 | tf_op jit(solution)/shard_map/all_to_all | solution.py:409
  53.9 10.4 %collective-permute-done.3.far_ref = bf16[3072,128]{1,0:T(8,128)(2,1)S(1)} collective-permute-done((bf16[3072,128]{1,0:T(8,128)(2,1)S(1)}, bf16[3072,128]{1,0:T(8,128)(2,1)S(1)}, u32[]{:S(2)}, u32[]{:S(2)}) %collective-permute-start.3) | collective-permute-done | bytes 786464 | tf_op jit(solution)/shard_map/ppermute | solution.py:408
  64.3 0.0 copy-start.1
  64.3 1.1 %copy-done.1 = bf16[3072,128]{1,0:T(8,128)(2,1)S(1)} copy-done((bf16[3072,128]{1,0:T(8,128)(2,1)S(1)}, bf16[3072,128]{1,0:T(8,128)(2,1)}, u32[]{:S(2)}) %copy-start.1) | copy-done | bytes 786456
  65.4 2.0 %own_sum.1 = (f32[3072,128]{1,0:T(8,128)S(1)}, bf16[256,2048]{1,0:T(8,128)(2,1)S(1)}, s32[16,128]{1,0:T(8,128)S(1)}) custom-call(s32[64,2,2,128]{3,2,1,0:T(2,128)} %bitcast.2.given_ref.ints_ref, bf16[3072,128]{1,0:T(8,128)(2,1)S(1)} %copy-done.1, bf16[3072,256]{1,0:T(8,128)(2,1)} %collective-permute-done.2.core_ref, ...), custom_call_target="tpu_custom_call" | custom-call | flops 199999995904 | bytes 67108864 | tf_op jit(solution)/shard_map/own_sum/pallas_call | solution.py:330
  67.5 16.8 %all-to-all-done.1 = bf16[128,32,128]{2,1,0:T(8,128)(2,1)} async-done(((bf16[128,32,128]{2,1,0:T(8,128)(2,1)}), bf16[128,32,128]{2,1,0:T(8,128)(2,1)}, u32[]{:S(2)}, u32[]{:S(2)}) %all-to-all-start.1) | async-done | bytes 1048608 | tf_op jit(solution)/shard_map/all_to_all | solution.py:409
  84.3 6.7 %scatter_sum.1 = bf16[3072,128]{1,0:T(8,128)(2,1)} custom-call(bf16[256,2048]{1,0:T(8,128)(2,1)S(1)} %get-tuple-element.29.low_ref, s32[16,128]{1,0:T(8,128)S(1)} %get-tuple-element.30.high_ref, f32[3072,128]{1,0:T(8,128)S(1)} %get-tuple-element.31.own_ref, bf16[64,2,32,128]{3,2,1,0:T(8,128)(2,1)} %bitcast.4.came_ref), custom_call_target="tpu_custom_call" | custom-call | flops 1000 | bytes 1000 | tf_op jit(solution)/shard_map/scatter_sum/pallas_call | solution.py:374
Async XLA Ops:
  2.2 24.7 %all-to-all-start = ((s32[128,2,128]{2,1,0:T(2,128)}), s32[128,2,128]{2,1,0:T(2,128)}, u32[]{:S(2)}, u32[]{:S(2)}) async-start(s32[128,2,128]{2,1,0:T(2,128)} %bitcast.5), calls=%async_computation | async-start | bytes 262144 | tf_op jit(solution)/shard_map/all_to_all | solution.py:399
  16.6 10.3 %collective-permute-start.1 = (bf16[1280,512]{1,0:T(8,128)(2,1)}, bf16[1280,512]{1,0:T(8,128)(2,1)}, u32[]{:S(2)}, u32[]{:S(2)}) collective-permute-start(bf16[1280,512]{1,0:T(8,128)(2,1)} %probe_ref.3), channel_id=1, source_target_pairs={{0,1},{1,0},{2,3},{3,2},{4,5},{5,4},{6,7},{7,6},{8,9},{9,8},{10,11... | collective-permute-start | bytes 3932168 | tf_op jit(solution)/shard_map/ppermute | solution.py:397
  16.8 10.1 %collective-permute-start = (bf16[2048,512]{1,0:T(8,128)(2,1)}, bf16[2048,512]{1,0:T(8,128)(2,1)}, u32[]{:S(2)}, u32[]{:S(2)}) collective-permute-start(bf16[2048,512]{1,0:T(8,128)(2,1)} %x_ref.3), channel_id=1, source_target_pairs={{0,1},{1,0},{2,3},{3,2},{4,5},{5,4},{6,7},{7,6},{8,9},{9,8},{10,11... | collective-permute-start | bytes 6291464 | tf_op jit(solution)/shard_map/ppermute | solution.py:396
  26.9 10.3 %collective-permute-start.2 = (bf16[3072,256]{1,0:T(8,128)(2,1)}, bf16[3072,256]{1,0:T(8,128)(2,1)}, u32[]{:S(2)}, u32[]{:S(2)}) collective-permute-start(bf16[3072,256]{1,0:T(8,128)(2,1)} %get-tuple-element.26), channel_id=1, source_target_pairs={{0,1},{1,0},{2,3},{3,2},{4,5},{5,4},{6,7},{7,6},{8,9},{9,8},{10,11... | collective-permute-start | bytes 4718600 | tf_op jit(solution)/shard_map/ppermute | solution.py:404
  27.1 10.2 %copy-start = (bf16[3072,128]{1,0:T(8,128)(2,1)S(1)}, bf16[3072,128]{1,0:T(8,128)(2,1)}, u32[]{:S(2)}) copy-start(bf16[3072,128]{1,0:T(8,128)(2,1)} %get-tuple-element.28.keep_ref) | copy-start | bytes 2359300
  38.8 25.5 %collective-permute-start.3 = (bf16[3072,128]{1,0:T(8,128)(2,1)S(1)}, bf16[3072,128]{1,0:T(8,128)(2,1)S(1)}, u32[]{:S(2)}, u32[]{:S(2)}) collective-permute-start(bf16[3072,128]{1,0:T(8,128)(2,1)S(1)} %core_sum.1), channel_id=1, source_target_pairs={{0,2},{2,0},{1,3},{3,1},{4,6},{6,4},{5,7},{7,5},{8,10},{10,8},{9,1... | collective-permute-start | bytes 2359304 | tf_op jit(solution)/shard_map/ppermute | solution.py:408
  41.1 43.3 %all-to-all-start.1 = ((bf16[128,32,128]{2,1,0:T(8,128)(2,1)}), bf16[128,32,128]{2,1,0:T(8,128)(2,1)}, u32[]{:S(2)}, u32[]{:S(2)}) async-start(bf16[128,32,128]{2,1,0:T(8,128)(2,1)} %bitcast.3), calls=%async_computation.1 | async-start | bytes 2097152 | tf_op jit(solution)/shard_map/all_to_all | solution.py:409
  64.3 1.1 %copy-start.1 = (bf16[3072,128]{1,0:T(8,128)(2,1)S(1)}, bf16[3072,128]{1,0:T(8,128)(2,1)}, u32[]{:S(2)}) copy-start(bf16[3072,128]{1,0:T(8,128)(2,1)} %get-tuple-element.22.keep_ref) | copy-start | bytes 2359300

commit v2 on v1

--- a/solution.py
+++ b/solution.py
@@ -30,7 +30,7 @@
     return target, child_map - target * ROWS
 
 
-def rank_kernel(map_ref, mask_ref, pos_ref, out_ref, hot_ref, val_ref):
+def rank_kernel(map_ref, mask_ref, mask2_ref, pos_ref, out_ref, hot_ref, val_ref):
     target, place = split_map(map_ref[...])
     blocks = KIDS // LANES
     upper = (iota((LANES, 2 * LANES), 0) < iota((LANES, 2 * LANES), 1)).astype(F32).astype(BF)
@@ -53,30 +53,30 @@
         hot_ref[...], val_ref[...], (((1,), (1,)), ((), ())), preferred_element_type=F32
     )
     places = (both[:, :LANES] * 64.0 + both[:, LANES:]).astype(I32)
-    lane = iota((12, LANES), 1) & 63
+    lane = iota((12, LANES), 1)
     row = iota((12, LANES), 0)
     flat = jnp.zeros((1, LANES), I32)
-    for t in range(4):
-        flat += jnp.sum(
-            jnp.where(lane == row * 4 + t, mask_ref[:, t : t + 1], 0), axis=0, keepdims=True
-        )
-    for core in range(2):
-        out_ref[:, core, 0, :] = places
-        out_ref[:, core, 1, :] = jnp.broadcast_to(flat, (WIDE, LANES))
-
-
-def rank_call(child_map, tile_mask):
+    for first, ref in ((0, mask_ref), (64, mask2_ref)):
+        for t in range(4):
+            flat += jnp.sum(
+                jnp.where(lane == first + row * 4 + t, ref[:, t : t + 1], 0), axis=0, keepdims=True
+            )
+    out_ref[:, 0, :] = places
+    out_ref[:, 1, :] = jnp.broadcast_to(flat, (WIDE, LANES))
+
+
+def rank_call(child_map, tile_mask, tile_mask2):
     return pl.pallas_call(
         rank_kernel,
         out_shape=(
             jax.ShapeDtypeStruct((KIDS // LANES, LANES), I32),
-            jax.ShapeDtypeStruct((WIDE, 2, 2, LANES), I32),
+            jax.ShapeDtypeStruct((WIDE, 2, LANES), I32),
         ),
         scratch_shapes=[pltpu.VMEM((WIDE, KIDS), BF), pltpu.VMEM((2 * LANES, KIDS), BF)],
         compiler_params=params(58),
         cost_estimate=pl.CostEstimate(flops=1000, bytes_accessed=1000, transcendentals=0),
         name="rank",
-    )(child_map, tile_mask)
+    )(child_map, tile_mask, tile_mask2)
 
 
 def load_probes(src, dst, sem, starts, first=0, first_sem=0):
@@ -95,8 +95,8 @@
 
 
 def parent_kernel(
-    mask_ref, x_ref, probe_ref, far_keep_ref, own_keep_ref, send_ref,
-    held_ref, buf_ref, out_ref, probe_sem, sems, out_sems,
+    mask_hbm, x_ref, probe_ref, far_keep_ref, own_keep_ref, send_ref,
+    held_ref, buf_ref, out_ref, mask_ref, mask_sem, probe_sem, sems, out_sems,
 ):
     h, c = lax.axis_index("h"), lax.axis_index("c")
     tall = PARENT_TALL
@@ -114,9 +114,10 @@
         for k in range(ROWS // 256)
     ]
     step = tall // 256
-    for copy in probe_copies + reads[: 2 * step]:
+    mask_copy = pltpu.make_async_copy(mask_hbm, mask_ref, mask_sem)
+    for copy in [mask_copy] + probe_copies + reads[: 2 * step]:
         copy.start()
-    for copy in probe_copies:
+    for copy in [mask_copy] + probe_copies:
         copy.wait()
     writes = []
     for k in range(chunks):
@@ -158,7 +159,6 @@
 
 
 VM = pl.BlockSpec(memory_space=pltpu.VMEM)
-SM = pl.BlockSpec(memory_space=pltpu.SMEM)
 ANY = pl.BlockSpec(memory_space=pl.ANY)
 LONG = pl.CostEstimate(flops=200 * 10**9, bytes_accessed=64 * MIB, transcendentals=0)
 SHORT = pl.CostEstimate(flops=1000, bytes_accessed=1000, transcendentals=0)
@@ -167,7 +167,7 @@
 def parent_call(tile_mask, front, probes):
     return pl.pallas_call(
         parent_kernel,
-        in_specs=[SM, ANY, ANY],
+        in_specs=[ANY] * 3,
         out_specs=[ANY] * 3,
         out_shape=[
             jax.ShapeDtypeStruct((ROWS, LANES), BF),
@@ -178,6 +178,8 @@
             pltpu.VMEM((1280, 512), BF),
             pltpu.VMEM((ROWS, 1280), BF),
             pltpu.VMEM((ROWS, 512), BF),
+            pltpu.SMEM((12, 10), I32),
+            pltpu.SemaphoreType.DMA,
             pltpu.SemaphoreType.DMA((4,)),
             pltpu.SemaphoreType.DMA((ROWS // 256,)),
             pltpu.SemaphoreType.DMA((ROWS // PARENT_TALL, 3)),
@@ -189,9 +191,9 @@
 
 
 def child_kernel(
-    map_ref, pos_ref, given_ref, x_ref, other_ref, probe_ref, probe2_ref,
+    map_hbm, pos_hbm, given_hbm, x_ref, other_ref, probe_ref, probe2_ref,
     out_ref, held_ref, buf_ref, hot_ref, low_ref, product_ref, perm_ref, stage_ref,
-    probe_sem, sems, out_sems,
+    map_ref, pos_ref, given_ref, small_sem, probe_sem, sems, out_sems,
 ):
     c = lax.axis_index("c")
     tall = 1024
@@ -208,24 +210,27 @@
                     src.at[at], buf_ref.at[at, pl.ds(n * 512, 512)], sems.at[k, n]
                 )
             )
-    for copy in copies + reads:
+    small = [
+        pltpu.make_async_copy(src, dst, small_sem.at[k])
+        for k, (src, dst) in enumerate(
+            ((map_hbm, map_ref), (given_hbm, given_ref), (pos_hbm, pos_ref))
+        )
+    ]
+    for copy in small + reads[:4] + copies + reads[4:]:
         copy.start()
+    small[0].wait()
 
     target, place = split_map(map_ref[...])
     tile = place >> 8
-    pos = pos_ref[...]
-    low = pos & 255
     for b in range(KIDS // LANES):
         rows = slice(b * LANES, (b + 1) * LANES)
         hot = (iota((LANES, LANES), 0) == target[b : b + 1, :]).astype(F32)
         hot_ref[rows, :LANES] = hot.T.astype(BF)
         on = (((iota((LANES, LANES), 0) & 63) >> 2) == tile[b : b + 1, :]).astype(F32)
         hot_ref[rows, LANES:] = on.T.astype(BF)
-        low_ref[:, rows] = (iota((256, LANES), 0) == low[b : b + 1, :]).astype(F32).astype(BF)
-
-    own = given_ref[:, pl.ds(c, 1), 1, :].reshape(WIDE, LANES)
-    other = given_ref[:, pl.ds(1 - c, 1), 1, :].reshape(WIDE, LANES)
-    mask = jnp.where(iota((WIDE, LANES), 1) < 64, own, other).astype(F32).astype(BF)
+
+    small[1].wait()
+    mask = given_ref[:, 1, :].astype(F32).astype(BF)
     mask = jnp.concatenate([mask, jnp.zeros((WIDE, LANES), BF)], axis=0)
     lane, col = iota((LANES, 1024), 0), iota((LANES, 1024), 1)
     expand = ((lane >> 6) * 4 + (lane & 3) == (col >> 7)).astype(F32).astype(BF)
@@ -242,7 +247,13 @@
         product_ref[rows, :] = jnp.dot(
             buf_ref[rows, :] * row_mask, held_ref[...], preferred_element_type=F32
         ).astype(BF)
-    high = pos >> 8
+    small[2].wait()
+    pos = pos_ref[...]
+    low, high = pos & 255, pos >> 8
+    for b in range(KIDS // LANES):
+        low_ref[:, b * LANES : (b + 1) * LANES] = (
+            (iota((256, LANES), 0) == low[b : b + 1, :]).astype(F32).astype(BF)
+        )
     writes = []
     for k in range(KIDS // tall):
         for q in range(tall // 256):
@@ -267,7 +278,7 @@
 def child_call(child_map, pos, given, rows, other, probes, probes2):
     return pl.pallas_call(
         child_kernel,
-        in_specs=[VM, VM, VM, ANY, ANY, ANY, ANY],
+        in_specs=[ANY] * 7,
         out_specs=ANY,
         out_shape=jax.ShapeDtypeStruct((WIDE, 2, PAIR, LANES), BF),
         scratch_shapes=[
@@ -278,6 +289,10 @@
             pltpu.VMEM((KIDS, 256), BF),
             pltpu.VMEM((2, 1024, KIDS), BF),
             pltpu.VMEM((WIDE, 2, PAIR, LANES), BF),
+            pltpu.VMEM((KIDS // LANES, LANES), I32),
+            pltpu.VMEM((KIDS // LANES, LANES), I32),
+            pltpu.VMEM((WIDE, 2, LANES), I32),
+            pltpu.SemaphoreType.DMA((3,)),
             pltpu.SemaphoreType.DMA((4,)),
             pltpu.SemaphoreType.DMA((4, 2)),
             pltpu.SemaphoreType.DMA((2,)),
@@ -292,7 +307,7 @@
     lane = iota((KIDS // LANES, LANES), 1) >> 5
     out = jnp.zeros((KIDS // LANES, LANES), I32)
     for q in range(4):
-        out = jnp.where(lane == q, ints_ref[pl.ds(q, KIDS // LANES, stride=4), 0, 0, :], out)
+        out = jnp.where(lane == q, ints_ref[pl.ds(q, KIDS // LANES, stride=4), 0, :], out)
     return out
 
 
@@ -317,13 +332,13 @@
         keep_ref[...].astype(F32) + core_ref[:, LANES:].astype(F32) + far_ref[...].astype(F32)
     )
     place = gather_lanes(ints_ref)
-    high_ref[...] = place >> 8
+    high = (place >> 8).astype(F32)
     low = place & 255
     row = iota((256, LANES), 0)
     for b in range(KIDS // LANES):
-        low_ref[:, b * LANES : (b + 1) * LANES] = (
-            (low[b : b + 1, :] == row).astype(F32).astype(BF)
-        )
+        at = slice(b * LANES, (b + 1) * LANES)
+        low_ref[:, at] = (low[b : b + 1, :] == row).astype(F32).astype(BF)
+        high_ref[at, :] = jnp.broadcast_to(high[b : b + 1, :], (LANES, LANES)).T.astype(BF)
 
 
 def own_call(ints, keep, core, far):
@@ -334,7 +349,7 @@
         out_shape=[
             jax.ShapeDtypeStruct((ROWS, LANES), F32),
             jax.ShapeDtypeStruct((256, KIDS), BF),
-            jax.ShapeDtypeStruct((KIDS // LANES, LANES), I32),
+            jax.ShapeDtypeStruct((KIDS, LANES), BF),
         ],
         compiler_params=params(8),
         cost_estimate=LONG,
@@ -343,26 +358,25 @@
 
 
 def final_kernel(
-    low_ref, high_ref, own_ref, came_ref, out_ref, held_ref, hot_ref, stage_ref, out_sems
+    low_ref, high_ref, own_ref, came_ref, out_ref, sum_ref, part_ref, stage_ref, out_sems
 ):
     for w in range(WIDE):
-        for half in range(2):
-            held_ref[w * PAIR : (w + 1) * PAIR, half * LANES : (half + 1) * LANES] = came_ref[
-                w, half
-            ]
-    high = high_ref[...]
-    tall = 1024
+        sum_ref[w * PAIR : (w + 1) * PAIR, :] = (
+            came_ref[w, 0].astype(F32) + came_ref[w, 1].astype(F32)
+        ).astype(BF)
     writes = []
-    for k in range(ROWS // tall):
-        for q in range(tall // 256):
-            on = (high == k * (tall // 256) + q).astype(F32).astype(BF)
-            for b in range(KIDS // LANES):
-                at = slice(b * LANES, (b + 1) * LANES)
-                hot_ref[k % 2, q * 256 : (q + 1) * 256, at] = low_ref[:, at] * on[b : b + 1, :]
-        added = jnp.dot(hot_ref[k % 2], held_ref[...], preferred_element_type=F32)
-        rows = slice(k * tall, (k + 1) * tall)
-        stage_ref[rows, :] = (own_ref[rows, :] + (added[:, :LANES] + added[:, LANES:])).astype(BF)
-        at = pl.ds(k * tall, tall)
+    for k in range(ROWS // 512):
+        for q in range(2):
+            part_ref[k % 2, :, q * LANES : (q + 1) * LANES] = jnp.where(
+                high_ref[...] == 2 * k + q, sum_ref[...], jnp.zeros((), BF)
+            )
+        added = jnp.dot(low_ref[...], part_ref[k % 2], preferred_element_type=F32)
+        for q in range(2):
+            rows = slice((2 * k + q) * 256, (2 * k + q + 1) * 256)
+            stage_ref[rows, :] = (
+                own_ref[rows, :] + added[:, q * LANES : (q + 1) * LANES]
+            ).astype(BF)
+        at = pl.ds(k * 512, 512)
         copy = pltpu.make_async_copy(stage_ref.at[at], out_ref.at[at], out_sems.at[k])
         copy.start()
         writes.append(copy)
@@ -377,10 +391,10 @@
         out_specs=ANY,
         out_shape=jax.ShapeDtypeStruct((ROWS, LANES), BF),
         scratch_shapes=[
-            pltpu.VMEM((KIDS, 256), BF),
-            pltpu.VMEM((2, 1024, KIDS), BF),
+            pltpu.VMEM((KIDS, LANES), BF),
+            pltpu.VMEM((2, KIDS, 256), BF),
             pltpu.VMEM((ROWS, LANES), BF),
-            pltpu.SemaphoreType.DMA((3,)),
+            pltpu.SemaphoreType.DMA((ROWS // 512,)),
         ],
         compiler_params=params(20),
         cost_estimate=SHORT,
@@ -395,10 +409,8 @@
     child_map = child_map.reshape(KIDS // LANES, LANES)
     other = lax.ppermute(child_updates, "c", SWAP)
     probes2 = lax.ppermute(probes, "c", SWAP)
-    pos, mine = rank_call(child_map, tile_mask)
-    given = lax.all_to_all(
-        mine.reshape(2 * WIDE, 2, LANES), WIDE_AXES + ("c",), split_axis=0, concat_axis=0, tiled=True
-    ).reshape(WIDE, 2, 2, LANES)
+    pos, mine = rank_call(child_map, tile_mask, lax.ppermute(tile_mask, "c", SWAP))
+    given = lax.all_to_all(mine, WIDE_AXES, split_axis=0, concat_axis=0, tiled=True)
     far_keep, own_keep, send = parent_call(tile_mask, parent_front, probes)
     given, other, probes2, send = lax.optimization_barrier((given, other, probes2, send))
     core = lax.ppermute(send, "c", SWAP)

time: 91.7 us -> 89.3 us (0.974)
  local copies, waits for them, and re-layouts: 1.14 us -> 3.75 us
  starting transfers between devices: 30.1 us -> 28 us
  Pallas kernels: 31.7 us -> 29.7 us
    all_to_all x1, waiting for transfers between devices: 16.8 us -> 13.4 us  [local(): lax.all_to_all(kid.reshape(2 * WIDE, PAIR, LANES), WIDE_AXES + ('h',), sp...]
    unnamed x4 -> x10, local copies, waits for them, and re-layouts: 1.14 us -> 3.75 us
    pallas_call x1, Pallas kernels: 6.7 us -> 4.94 us  [final_call(): pl.pallas_call(final_kernel, in_specs=[VM] * 4, out_specs=ANY, out_shape=...]
    all_to_all x1, starting transfers between devices: 14.4 us -> 13.3 us  [local(): lax.all_to_all(mine, WIDE_AXES, split_axis=0, concat_axis=0, tiled=True)]
    ppermute x1, waiting for transfers between devices: 10.4 us -> 11.5 us  [local(): far = lax.ppermute(crossing, 'h', SWAP)]
  transfers between devices with their start and end apart: 6 -> 7, of which waited for: 3 -> 4; matrix products, arithmetic and copies ran while one was open for 0% -> 0% of each run, Pallas kernels for 23% -> 26%
where the time goes in v2:
time: 89.3 us; the launch traced here: 88.9 us
  Pallas kernels  29.7 us (33%)
  starting transfers between devices  28 us (31%)
  waiting for transfers between devices  27.1 us (30%)
  local copies, waits for them, and re-layouts  3.75 us (4%)
    all_to_all x1, waiting for transfers between devices, local(): lax.all_to_all(kid.reshape(2 * WIDE, PAIR, LANES), WIDE_AXES + ('h',), sp...  13.4 us
    all_to_all x1, starting transfers between devices, local(): lax.all_to_all(mine, WIDE_AXES, split_axis=0, concat_axis=0, tiled=True)  13.3 us
    all_to_all x1, starting transfers between devices, local(): lax.all_to_all(kid.reshape(2 * WIDE, PAIR, LANES), WIDE_AXES + ('h',), sp...  12 us
    ppermute x1, waiting for transfers between devices, local(): far = lax.ppermute(crossing, 'h', SWAP)  11.5 us
    pallas_call x1, Pallas kernels, child_call(): pl.pallas_call(child_kernel, in_specs=[ANY] * 7, out_specs=ANY, out_shape...  10.3 us
    pallas_call x1, Pallas kernels, parent_call(): pl.pallas_call(parent_kernel, in_specs=[ANY] * 3, out_specs=[ANY] * 3, ou...  8.18 us
    pallas_call x1, Pallas kernels, final_call(): pl.pallas_call(final_kernel, in_specs=[VM] * 4, out_specs=ANY, out_shape=...  4.94 us
    unnamed x10, local copies, waits for them, and re-layouts  3.75 us
  transfers between devices with their start and end apart: 7, of which 4 were waited for; matrix products, arithmetic and copies ran while one was open for 0% of the time, Pallas kernels for 26%

profile of v2, /device:TPU:2, one launch (start us, length us, event | category | flops | bytes accessed | tf_op | source)
XLA Modules:
  0.0 88.9 jit_solution(2365927235557816723)
XLA Ops:
  0.0 0.0 collective-permute-start
  0.0 0.5 collective-permute-start.2
  0.5 0.0 collective-permute-start.1
  0.5 0.9 collective-permute-done.mask2_ref
  1.4 0.0 copy-start.4
  1.4 0.6 copy-done.4
  2.0 2.2 %rank.1 = (s32[16,128]{1,0:T(8,128)}, s32[64,2,128]{2,1,0:T(2,128)}) custom-call(s32[16,128]{1,0:T(8,128)} %bitcast.3, s32[12,10]{1,0:T(8,128)} %mask_hbm.1, s32[12,10]{1,0:T(8,128)} %copy-done.4), custom_call_target="tpu_custom_call" | custom-call | flops 1000 | bytes 1000 | tf_op jit(solution)/shard_map/rank/pallas_call | solution.py:69
  4.2 13.3 %all-to-all-start = ((s32[64,2,128]{2,1,0:T(2,128)}), s32[64,2,128]{2,1,0:T(2,128)}, u32[]{:S(2)}, u32[]{:S(2)}) async-start(s32[64,2,128]{2,1,0:T(2,128)} %get-tuple-element.19), calls=%async_computation | async-start | bytes 131072 | tf_op jit(solution)/shard_map/all_to_all | solution.py:413
  17.5 8.2 %parent_product.1 = (bf16[3072,128]{1,0:T(8,128)(2,1)}, bf16[3072,128]{1,0:T(8,128)(2,1)}, bf16[3072,256]{1,0:T(8,128)(2,1)}) custom-call(s32[12,10]{1,0:T(8,128)} %mask_hbm.1, bf16[3072,1280]{1,0:T(8,128)(2,1)} %x_ref.2, bf16[1280,512]{1,0:T(8,128)(2,1)} %probe_ref.3), custom_call_target="tpu_custom_call" | custom-call | flops 199999995904 | bytes 67108864 | tf_op jit(solution)/shard_map/parent_product/pallas_call | solution.py:168
  25.7 1.4 %all-to-all-done.given_hbm.ints_ref = s32[64,2,128]{2,1,0:T(2,128)} async-done(((s32[64,2,128]{2,1,0:T(2,128)}), s32[64,2,128]{2,1,0:T(2,128)}, u32[]{:S(2)}, u32[]{:S(2)}) %all-to-all-start) | async-done | bytes 65568 | tf_op jit(solution)/shard_map/all_to_all | solution.py:413
  27.0 0.0 collective-permute-done.2.probe2_ref
  27.0 0.0 collective-permute-done.1.other_ref
  27.0 0.0 collective-permute-start.3
  27.1 0.0 copy-start
  27.1 10.3 %child_product.1 = bf16[64,2,32,128]{3,2,1,0:T(8,128)(2,1)} custom-call(s32[16,128]{1,0:T(8,128)} %bitcast.4, s32[16,128]{1,0:T(8,128)} %get-tuple-element.23.pos_hbm, s32[64,2,128]{2,1,0:T(2,128)} %all-to-all-done.given_hbm.ints_ref, bf16[2048,512]{1,0:T(8,128)(2,1)} %x_ref.3, bf16[2048,512]{1,0:T(8,128)(2,1)} %collective-permute-done.1.other_ref, ...), custom_call_target="tpu_custom_call" | custom-call | flops 199999995904 | bytes 67108864 | tf_op jit(solution)/shard_map/child_product/pallas_call | solution.py:279
  37.4 0.0 collective-permute-done.3.core_ref
  37.4 0.0 copy-done
  37.4 1.6 %core_sum.1 = bf16[3072,128]{1,0:T(8,128)(2,1)S(1)} custom-call(bf16[3072,128]{1,0:T(8,128)(2,1)S(1)} %copy-done, bf16[3072,256]{1,0:T(8,128)(2,1)} %collective-permute-done.3.core_ref), custom_call_target="tpu_custom_call" | custom-call | flops 1000 | bytes 1000 | tf_op jit(solution)/shard_map/core_sum/pallas_call | solution.py:319
  39.0 2.2 %collective-permute-start.4 = (bf16[3072,128]{1,0:T(8,128)(2,1)S(1)}, bf16[3072,128]{1,0:T(8,128)(2,1)S(1)}, u32[]{:S(2)}, u32[]{:S(2)}) collective-permute-start(bf16[3072,128]{1,0:T(8,128)(2,1)S(1)} %core_sum.1), channel_id=1, source_target_pairs={{0,2},{2,0},{1,3},{3,1},{4,6},{6,4},{5,7},{7,5},{8,10},{10,8},{9,1... | collective-permute-start | bytes 2359304 | tf_op jit(solution)/shard_map/ppermute | solution.py:420
  41.2 12.0 %all-to-all-start.1 = ((bf16[128,32,128]{2,1,0:T(8,128)(2,1)}), bf16[128,32,128]{2,1,0:T(8,128)(2,1)}, u32[]{:S(2)}, u32[]{:S(2)}) async-start(bf16[128,32,128]{2,1,0:T(8,128)(2,1)} %bitcast.1), calls=%async_computation.1 | async-start | bytes 2097152 | tf_op jit(solution)/shard_map/all_to_all | solution.py:421
  53.2 11.5 %collective-permute-done.4.far_ref = bf16[3072,128]{1,0:T(8,128)(2,1)S(1)} collective-permute-done((bf16[3072,128]{1,0:T(8,128)(2,1)S(1)}, bf16[3072,128]{1,0:T(8,128)(2,1)S(1)}, u32[]{:S(2)}, u32[]{:S(2)}) %collective-permute-start.4) | collective-permute-done | bytes 786464 | tf_op jit(solution)/shard_map/ppermute | solution.py:420
  64.6 0.0 copy-start.1
  64.6 0.9 copy-done.1
  65.5 0.0 copy-start.2
  65.5 1.1 %copy-done.2 = bf16[3072,128]{1,0:T(8,128)(2,1)S(1)} copy-done((bf16[3072,128]{1,0:T(8,128)(2,1)S(1)}, bf16[3072,128]{1,0:T(8,128)(2,1)}, u32[]{:S(2)}) %copy-start.2) | copy-done | bytes 786456
  66.6 0.0 copy-start.3
  66.6 1.1 %copy-done.3 = bf16[3072,128]{1,0:T(8,128)(2,1)S(1)} copy-done((bf16[3072,128]{1,0:T(8,128)(2,1)S(1)}, bf16[3072,128]{1,0:T(8,128)(2,1)}, u32[]{:S(2)}) %copy-start.3) | copy-done | bytes 786456
  67.8 2.6 %own_sum.1 = (f32[3072,128]{1,0:T(8,128)S(1)}, bf16[256,2048]{1,0:T(8,128)(2,1)S(1)}, bf16[2048,128]{1,0:T(8,128)(2,1)S(1)}) custom-call(s32[64,2,128]{2,1,0:T(2,128)} %all-to-all-done.given_hbm.ints_ref, bf16[3072,128]{1,0:T(8,128)(2,1)S(1)} %copy-done.3, bf16[3072,256]{1,0:T(8,128)(2,1)} %collective-permute-done.3.core_ref, bf16[3072,128]{1,0:T(8,128)(2,1)S(1)} %copy-done.2), custom_call_target="tpu_custom_call" | custom-call | flops 199999995904 | bytes 67108864 | tf_op jit(solution)/shard_map/own_sum/pallas_call | solution.py:345
  70.3 13.4 %all-to-all-done.1 = bf16[128,32,128]{2,1,0:T(8,128)(2,1)} async-done(((bf16[128,32,128]{2,1,0:T(8,128)(2,1)}), bf16[128,32,128]{2,1,0:T(8,128)(2,1)}, u32[]{:S(2)}, u32[]{:S(2)}) %all-to-all-start.1) | async-done | bytes 1048608 | tf_op jit(solution)/shard_map/all_to_all | solution.py:421
  83.8 4.9 %scatter_sum.1 = bf16[3072,128]{1,0:T(8,128)(2,1)} custom-call(bf16[256,2048]{1,0:T(8,128)(2,1)S(1)} %get-tuple-element.29.low_ref, bf16[2048,128]{1,0:T(8,128)(2,1)S(1)} %get-tuple-element.30.high_ref, f32[3072,128]{1,0:T(8,128)S(1)} %get-tuple-element.31.own_ref, bf16[64,2,32,128]{3,2,1,0:T(8,128)(2,1)} %bitcast.2.came_ref), custom_call_target="tpu_custom_call" | custom-call | flops 1000 | bytes 1000 | tf_op jit(solution)/shard_map/scatter_sum/pallas_call | solution.py:388
Async XLA Ops:
  0.0 1.4 %collective-permute-start = (s32[12,10]{1,0:T(8,128)}, s32[12,10]{1,0:T(8,128)S(1)}, u32[]{:S(2)}, u32[]{:S(2)}) collective-permute-start(s32[12,10]{1,0:T(8,128)} %mask_hbm.1), channel_id=1, source_target_pairs={{0,1},{1,0},{2,3},{3,2},{4,5},{5,4},{6,7},{7,6},{8,9},{9,8},{10,11... | collective-permute-start | bytes 1448 | tf_op jit(solution)/shard_map/ppermute | solution.py:412
  0.0 27.0 %collective-permute-start.2 = (bf16[1280,512]{1,0:T(8,128)(2,1)}, bf16[1280,512]{1,0:T(8,128)(2,1)}, u32[]{:S(2)}, u32[]{:S(2)}) collective-permute-start(bf16[1280,512]{1,0:T(8,128)(2,1)} %probe_ref.3), channel_id=1, source_target_pairs={{0,1},{1,0},{2,3},{3,2},{4,5},{5,4},{6,7},{7,6},{8,9},{9,8},{10,11... | collective-permute-start | bytes 3932168 | tf_op jit(solution)/shard_map/ppermute | solution.py:411
  0.5 26.5 %collective-permute-start.1 = (bf16[2048,512]{1,0:T(8,128)(2,1)}, bf16[2048,512]{1,0:T(8,128)(2,1)}, u32[]{:S(2)}, u32[]{:S(2)}) collective-permute-start(bf16[2048,512]{1,0:T(8,128)(2,1)} %x_ref.3), channel_id=1, source_target_pairs={{0,1},{1,0},{2,3},{3,2},{4,5},{5,4},{6,7},{7,6},{8,9},{9,8},{10,11... | collective-permute-start | bytes 6291464 | tf_op jit(solution)/shard_map/ppermute | solution.py:410
  1.4 0.6 copy-start.4
  4.2 22.9 %all-to-all-start = ((s32[64,2,128]{2,1,0:T(2,128)}), s32[64,2,128]{2,1,0:T(2,128)}, u32[]{:S(2)}, u32[]{:S(2)}) async-start(s32[64,2,128]{2,1,0:T(2,128)} %get-tuple-element.19), calls=%async_computation | async-start | bytes 131072 | tf_op jit(solution)/shard_map/all_to_all | solution.py:413
  27.0 10.3 %collective-permute-start.3 = (bf16[3072,256]{1,0:T(8,128)(2,1)}, bf16[3072,256]{1,0:T(8,128)(2,1)}, u32[]{:S(2)}, u32[]{:S(2)}) collective-permute-start(bf16[3072,256]{1,0:T(8,128)(2,1)} %get-tuple-element.26), channel_id=1, source_target_pairs={{0,1},{1,0},{2,3},{3,2},{4,5},{5,4},{6,7},{7,6},{8,9},{9,8},{10,11... | collective-permute-start | bytes 4718600 | tf_op jit(solution)/shard_map/ppermute | solution.py:416
  27.1 10.3 %copy-start = (bf16[3072,128]{1,0:T(8,128)(2,1)S(1)}, bf16[3072,128]{1,0:T(8,128)(2,1)}, u32[]{:S(2)}) copy-start(bf16[3072,128]{1,0:T(8,128)(2,1)} %get-tuple-element.28.keep_ref) | copy-start | bytes 2359300
  39.0 25.6 %collective-permute-start.4 = (bf16[3072,128]{1,0:T(8,128)(2,1)S(1)}, bf16[3072,128]{1,0:T(8,128)(2,1)S(1)}, u32[]{:S(2)}, u32[]{:S(2)}) collective-permute-start(bf16[3072,128]{1,0:T(8,128)(2,1)S(1)} %core_sum.1), channel_id=1, source_target_pairs={{0,2},{2,0},{1,3},{3,1},{4,6},{6,4},{5,7},{7,5},{8,10},{10,8},{9,1... | collective-permute-start | bytes 2359304 | tf_op jit(solution)/shard_map/ppermute | solution.py:420
  41.2 42.6 %all-to-all-start.1 = ((bf16[128,32,128]{2,1,0:T(8,128)(2,1)}), bf16[128,32,128]{2,1,0:T(8,128)(2,1)}, u32[]{:S(2)}, u32[]{:S(2)}) async-start(bf16[128,32,128]{2,1,0:T(8,128)(2,1)} %bitcast.1), calls=%async_computation.1 | async-start | bytes 2097152 | tf_op jit(solution)/shard_map/all_to_all | solution.py:421
  64.6 0.9 copy-start.1
  65.5 1.1 %copy-start.2 = (bf16[3072,128]{1,0:T(8,128)(2,1)S(1)}, bf16[3072,128]{1,0:T(8,128)(2,1)}, u32[]{:S(2)}) copy-start(bf16[3072,128]{1,0:T(8,128)(2,1)} %copy-done.1) | copy-start | bytes 2359300
  66.6 1.1 %copy-start.3 = (bf16[3072,128]{1,0:T(8,128)(2,1)S(1)}, bf16[3072,128]{1,0:T(8,128)(2,1)}, u32[]{:S(2)}) copy-start(bf16[3072,128]{1,0:T(8,128)(2,1)} %get-tuple-element.22.keep_ref) | copy-start | bytes 2359300

commit v3 on v2

--- a/solution.py
+++ b/solution.py
@@ -312,14 +312,16 @@
 
 
 def cross_kernel(keep_ref, core_ref, out_ref):
-    out_ref[...] = (keep_ref[...].astype(F32) + core_ref[:, :LANES].astype(F32)).astype(BF)
+    out_ref[...] = (keep_ref[...].astype(F32) + core_ref[...].astype(F32)).astype(BF)
 
 
 def cross_call(keep, core):
+    part = pl.BlockSpec((ROWS, LANES), lambda i: (0, 0))
     return pl.pallas_call(
         cross_kernel,
-        in_specs=[VM, VM],
-        out_specs=VM,
+        grid=(1,),
+        in_specs=[part, part],
+        out_specs=part,
         out_shape=jax.ShapeDtypeStruct((ROWS, LANES), BF),
         compiler_params=params(8),
         cost_estimate=SHORT,
@@ -330,7 +332,7 @@
 def own_kernel(ints_ref, keep_ref, core_ref, far_ref, out_ref, low_ref, high_ref):
     out_ref[...] = (
         keep_ref[...].astype(F32) + core_ref[:, LANES:].astype(F32) + far_ref[...].astype(F32)
-    )
+    ).astype(BF)
     place = gather_lanes(ints_ref)
     high = (place >> 8).astype(F32)
     low = place & 255
@@ -347,7 +349,7 @@
         in_specs=[VM] * 4,
         out_specs=[VM] * 3,
         out_shape=[
-            jax.ShapeDtypeStruct((ROWS, LANES), F32),
+            jax.ShapeDtypeStruct((ROWS, LANES), BF),
             jax.ShapeDtypeStruct((256, KIDS), BF),
             jax.ShapeDtypeStruct((KIDS, LANES), BF),
         ],
@@ -374,7 +376,7 @@
         for q in range(2):
             rows = slice((2 * k + q) * 256, (2 * k + q + 1) * 256)
             stage_ref[rows, :] = (
-                own_ref[rows, :] + added[:, q * LANES : (q + 1) * LANES]
+                own_ref[rows, :].astype(F32) + added[:, q * LANES : (q + 1) * LANES]
             ).astype(BF)
         at = pl.ds(k * 512, 512)
         copy = pltpu.make_async_copy(stage_ref.at[at], out_ref.at[at], out_sems.at[k])

time: 89.3 us -> 89 us (level)
  local copies, waits for them, and re-layouts: 3.75 us -> 1.74 us
  waiting for transfers between devices: 27.1 us -> 29 us
    unnamed x10 -> x6, local copies, waits for them, and re-layouts: 3.75 us -> 1.74 us
    all_to_all x1, waiting for transfers between devices: 13.4 us -> 15.3 us  [local(): lax.all_to_all(kid.reshape(2 * WIDE, PAIR, LANES), WIDE_AXES + ('h',), sp...]
where the time goes in v3:
time: 89 us; the launch traced here: 88.6 us
  Pallas kernels  29.6 us (33%)
  waiting for transfers between devices  29 us (33%)
  starting transfers between devices  28 us (31%)
  local copies, waits for them, and re-layouts  1.74 us (2%)
    all_to_all x1, waiting for transfers between devices, local(): lax.all_to_all(kid.reshape(2 * WIDE, PAIR, LANES), WIDE_AXES + ('h',), sp...  15.3 us
    all_to_all x1, starting transfers between devices, local(): lax.all_to_all(mine, WIDE_AXES, split_axis=0, concat_axis=0, tiled=True)  13.3 us
    all_to_all x1, starting transfers between devices, local(): lax.all_to_all(kid.reshape(2 * WIDE, PAIR, LANES), WIDE_AXES + ('h',), sp...  12 us
    ppermute x1, waiting for transfers between devices, local(): far = lax.ppermute(crossing, 'h', SWAP)  11.5 us
    pallas_call x1, Pallas kernels, child_call(): pl.pallas_call(child_kernel, in_specs=[ANY] * 7, out_specs=ANY, out_shape...  10.3 us
    pallas_call x1, Pallas kernels, parent_call(): pl.pallas_call(parent_kernel, in_specs=[ANY] * 3, out_specs=[ANY] * 3, ou...  8.17 us
    pallas_call x1, Pallas kernels, final_call(): pl.pallas_call(final_kernel, in_specs=[VM] * 4, out_specs=ANY, out_shape=...  4.94 us
    pallas_call x1, Pallas kernels, own_call(): pl.pallas_call(own_kernel, in_specs=[VM] * 4, out_specs=[VM] * 3, out_sha...  2.66 us
  transfers between devices with their start and end apart: 7, of which 4 were waited for; matrix products, arithmetic and copies ran while one was open for 0% of the time, Pallas kernels for 26%

profile of v3, /device:TPU:2, one launch (start us, length us, event | category | flops | bytes accessed | tf_op | source)
XLA Modules:
  0.0 88.6 jit_solution(3464073221634730219)
XLA Ops:
  0.0 0.0 collective-permute-start
  0.0 0.5 collective-permute-start.2
  0.5 0.0 collective-permute-start.1
  0.5 0.9 collective-permute-done.mask2_ref
  1.4 0.0 copy-start.2
  1.4 0.6 copy-done.2
  2.0 2.2 %rank.1 = (s32[16,128]{1,0:T(8,128)}, s32[64,2,128]{2,1,0:T(2,128)}) custom-call(s32[16,128]{1,0:T(8,128)} %bitcast.3, s32[12,10]{1,0:T(8,128)} %mask_hbm.1, s32[12,10]{1,0:T(8,128)} %copy-done.2), custom_call_target="tpu_custom_call" | custom-call | flops 1000 | bytes 1000 | tf_op jit(solution)/shard_map/rank/pallas_call | solution.py:69
  4.2 13.3 %all-to-all-start = ((s32[64,2,128]{2,1,0:T(2,128)}), s32[64,2,128]{2,1,0:T(2,128)}, u32[]{:S(2)}, u32[]{:S(2)}) async-start(s32[64,2,128]{2,1,0:T(2,128)} %get-tuple-element.19), calls=%async_computation | async-start | bytes 131072 | tf_op jit(solution)/shard_map/all_to_all | solution.py:415
  17.5 8.2 %parent_product.1 = (bf16[3072,128]{1,0:T(8,128)(2,1)}, bf16[3072,128]{1,0:T(8,128)(2,1)}, bf16[3072,256]{1,0:T(8,128)(2,1)}) custom-call(s32[12,10]{1,0:T(8,128)} %mask_hbm.1, bf16[3072,1280]{1,0:T(8,128)(2,1)} %x_ref.2, bf16[1280,512]{1,0:T(8,128)(2,1)} %probe_ref.3), custom_call_target="tpu_custom_call" | custom-call | flops 199999995904 | bytes 67108864 | tf_op jit(solution)/shard_map/parent_product/pallas_call | solution.py:168
  25.7 1.4 %all-to-all-done.given_hbm.ints_ref = s32[64,2,128]{2,1,0:T(2,128)} async-done(((s32[64,2,128]{2,1,0:T(2,128)}), s32[64,2,128]{2,1,0:T(2,128)}, u32[]{:S(2)}, u32[]{:S(2)}) %all-to-all-start) | async-done | bytes 65568 | tf_op jit(solution)/shard_map/all_to_all | solution.py:415
  27.0 0.0 collective-permute-done.2.probe2_ref
  27.0 0.0 collective-permute-done.1.other_ref
  27.0 0.0 collective-permute-start.3
  27.0 0.0 copy-start
  27.1 10.3 %child_product.1 = bf16[64,2,32,128]{3,2,1,0:T(8,128)(2,1)} custom-call(s32[16,128]{1,0:T(8,128)} %bitcast.4, s32[16,128]{1,0:T(8,128)} %get-tuple-element.23.pos_hbm, s32[64,2,128]{2,1,0:T(2,128)} %all-to-all-done.given_hbm.ints_ref, bf16[2048,512]{1,0:T(8,128)(2,1)} %x_ref.3, bf16[2048,512]{1,0:T(8,128)(2,1)} %collective-permute-done.1.other_ref, ...), custom_call_target="tpu_custom_call" | custom-call | flops 199999995904 | bytes 67108864 | tf_op jit(solution)/shard_map/child_product/pallas_call | solution.py:279
  37.4 0.0 collective-permute-done.3.core_ref
  37.4 0.0 copy-done
  37.4 1.3 %core_sum.1 = bf16[3072,128]{1,0:T(8,128)(2,1)S(1)} custom-call(bf16[3072,128]{1,0:T(8,128)(2,1)S(1)} %copy-done, bf16[3072,256]{1,0:T(8,128)(2,1)} %collective-permute-done.3.core_ref), custom_call_target="tpu_custom_call" | custom-call | flops 1000 | bytes 1000 | tf_op jit(solution)/shard_map/core_sum/pallas_call | solution.py:320
  38.7 2.2 %collective-permute-start.4 = (bf16[3072,128]{1,0:T(8,128)(2,1)S(1)}, bf16[3072,128]{1,0:T(8,128)(2,1)S(1)}, u32[]{:S(2)}, u32[]{:S(2)}) collective-permute-start(bf16[3072,128]{1,0:T(8,128)(2,1)S(1)} %core_sum.1), channel_id=1, source_target_pairs={{0,2},{2,0},{1,3},{3,1},{4,6},{6,4},{5,7},{7,5},{8,10},{10,8},{9,1... | collective-permute-start | bytes 2359304 | tf_op jit(solution)/shard_map/ppermute | solution.py:422
  40.9 12.0 %all-to-all-start.1 = ((bf16[128,32,128]{2,1,0:T(8,128)(2,1)}), bf16[128,32,128]{2,1,0:T(8,128)(2,1)}, u32[]{:S(2)}, u32[]{:S(2)}) async-start(bf16[128,32,128]{2,1,0:T(8,128)(2,1)} %bitcast.1), calls=%async_computation.1 | async-start | bytes 2097152 | tf_op jit(solution)/shard_map/all_to_all | solution.py:423
  52.9 11.5 %collective-permute-done.4.far_ref = bf16[3072,128]{1,0:T(8,128)(2,1)S(1)} collective-permute-done((bf16[3072,128]{1,0:T(8,128)(2,1)S(1)}, bf16[3072,128]{1,0:T(8,128)(2,1)S(1)}, u32[]{:S(2)}, u32[]{:S(2)}) %collective-permute-start.4) | collective-permute-done | bytes 786464 | tf_op jit(solution)/shard_map/ppermute | solution.py:422
  64.3 0.0 copy-start.1
  64.3 1.1 %copy-done.1 = bf16[3072,128]{1,0:T(8,128)(2,1)S(1)} copy-done((bf16[3072,128]{1,0:T(8,128)(2,1)S(1)}, bf16[3072,128]{1,0:T(8,128)(2,1)}, u32[]{:S(2)}) %copy-start.1) | copy-done | bytes 786456
  65.5 2.7 %own_sum.1 = (bf16[3072,128]{1,0:T(8,128)(2,1)S(1)}, bf16[256,2048]{1,0:T(8,128)(2,1)S(1)}, bf16[2048,128]{1,0:T(8,128)(2,1)S(1)}) custom-call(s32[64,2,128]{2,1,0:T(2,128)} %all-to-all-done.given_hbm.ints_ref, bf16[3072,128]{1,0:T(8,128)(2,1)S(1)} %copy-done.1, bf16[3072,256]{1,0:T(8,128)(2,1)} %collective-permute-done.3.core_ref, ...), custom_call_target="tpu_custom_call" | custom-call | flops 199999995904 | bytes 67108864 | tf_op jit(solution)/shard_map/own_sum/pallas_call | solution.py:347
  68.1 15.3 %all-to-all-done.1 = bf16[128,32,128]{2,1,0:T(8,128)(2,1)} async-done(((bf16[128,32,128]{2,1,0:T(8,128)(2,1)}), bf16[128,32,128]{2,1,0:T(8,128)(2,1)}, u32[]{:S(2)}, u32[]{:S(2)}) %all-to-all-start.1) | async-done | bytes 1048608 | tf_op jit(solution)/shard_map/all_to_all | solution.py:423
  83.5 4.9 %scatter_sum.1 = bf16[3072,128]{1,0:T(8,128)(2,1)} custom-call(bf16[256,2048]{1,0:T(8,128)(2,1)S(1)} %get-tuple-element.29.low_ref, bf16[2048,128]{1,0:T(8,128)(2,1)S(1)} %get-tuple-element.30.high_ref, bf16[3072,128]{1,0:T(8,128)(2,1)S(1)} %get-tuple-element.31.own_ref, bf16[64,2,32,128]{3,2,1,0:T(8,128)(2,1)} %bitcast.2.came_ref), custom_call_target="tpu_custom_call" | custom-call | flops 1000 | bytes 1000 | tf_op jit(solution)/shard_map/scatter_sum/pallas_call | solution.py:390
Async XLA Ops:
  0.0 1.4 %collective-permute-start = (s32[12,10]{1,0:T(8,128)}, s32[12,10]{1,0:T(8,128)S(1)}, u32[]{:S(2)}, u32[]{:S(2)}) collective-permute-start(s32[12,10]{1,0:T(8,128)} %mask_hbm.1), channel_id=1, source_target_pairs={{0,1},{1,0},{2,3},{3,2},{4,5},{5,4},{6,7},{7,6},{8,9},{9,8},{10,11... | collective-permute-start | bytes 1448 | tf_op jit(solution)/shard_map/ppermute | solution.py:414
  0.0 27.0 %collective-permute-start.2 = (bf16[1280,512]{1,0:T(8,128)(2,1)}, bf16[1280,512]{1,0:T(8,128)(2,1)}, u32[]{:S(2)}, u32[]{:S(2)}) collective-permute-start(bf16[1280,512]{1,0:T(8,128)(2,1)} %probe_ref.3), channel_id=1, source_target_pairs={{0,1},{1,0},{2,3},{3,2},{4,5},{5,4},{6,7},{7,6},{8,9},{9,8},{10,11... | collective-permute-start | bytes 3932168 | tf_op jit(solution)/shard_map/ppermute | solution.py:413
  0.5 26.5 %collective-permute-start.1 = (bf16[2048,512]{1,0:T(8,128)(2,1)}, bf16[2048,512]{1,0:T(8,128)(2,1)}, u32[]{:S(2)}, u32[]{:S(2)}) collective-permute-start(bf16[2048,512]{1,0:T(8,128)(2,1)} %x_ref.3), channel_id=1, source_target_pairs={{0,1},{1,0},{2,3},{3,2},{4,5},{5,4},{6,7},{7,6},{8,9},{9,8},{10,11... | collective-permute-start | bytes 6291464 | tf_op jit(solution)/shard_map/ppermute | solution.py:412
  1.4 0.6 copy-start.2
  4.2 22.9 %all-to-all-start = ((s32[64,2,128]{2,1,0:T(2,128)}), s32[64,2,128]{2,1,0:T(2,128)}, u32[]{:S(2)}, u32[]{:S(2)}) async-start(s32[64,2,128]{2,1,0:T(2,128)} %get-tuple-element.19), calls=%async_computation | async-start | bytes 131072 | tf_op jit(solution)/shard_map/all_to_all | solution.py:415
  27.0 10.3 %collective-permute-start.3 = (bf16[3072,256]{1,0:T(8,128)(2,1)}, bf16[3072,256]{1,0:T(8,128)(2,1)}, u32[]{:S(2)}, u32[]{:S(2)}) collective-permute-start(bf16[3072,256]{1,0:T(8,128)(2,1)} %get-tuple-element.26), channel_id=1, source_target_pairs={{0,1},{1,0},{2,3},{3,2},{4,5},{5,4},{6,7},{7,6},{8,9},{9,8},{10,11... | collective-permute-start | bytes 4718600 | tf_op jit(solution)/shard_map/ppermute | solution.py:418
  27.0 10.3 %copy-start = (bf16[3072,128]{1,0:T(8,128)(2,1)S(1)}, bf16[3072,128]{1,0:T(8,128)(2,1)}, u32[]{:S(2)}) copy-start(bf16[3072,128]{1,0:T(8,128)(2,1)} %get-tuple-element.28.keep_ref) | copy-start | bytes 2359300
  38.7 25.6 %collective-permute-start.4 = (bf16[3072,128]{1,0:T(8,128)(2,1)S(1)}, bf16[3072,128]{1,0:T(8,128)(2,1)S(1)}, u32[]{:S(2)}, u32[]{:S(2)}) collective-permute-start(bf16[3072,128]{1,0:T(8,128)(2,1)S(1)} %core_sum.1), channel_id=1, source_target_pairs={{0,2},{2,0},{1,3},{3,1},{4,6},{6,4},{5,7},{7,5},{8,10},{10,8},{9,1... | collective-permute-start | bytes 2359304 | tf_op jit(solution)/shard_map/ppermute | solution.py:422
  40.9 42.6 %all-to-all-start.1 = ((bf16[128,32,128]{2,1,0:T(8,128)(2,1)}), bf16[128,32,128]{2,1,0:T(8,128)(2,1)}, u32[]{:S(2)}, u32[]{:S(2)}) async-start(bf16[128,32,128]{2,1,0:T(8,128)(2,1)} %bitcast.1), calls=%async_computation.1 | async-start | bytes 2097152 | tf_op jit(solution)/shard_map/all_to_all | solution.py:423
  64.3 1.1 %copy-start.1 = (bf16[3072,128]{1,0:T(8,128)(2,1)S(1)}, bf16[3072,128]{1,0:T(8,128)(2,1)}, u32[]{:S(2)}) copy-start(bf16[3072,128]{1,0:T(8,128)(2,1)} %get-tuple-element.22.keep_ref) | copy-start | bytes 2359300
